TPU v7x, 256 devices: a whole 4x4x8 slice. The times are simulated.
256 devices in a mesh: qrow: 16 (over z_lo, x), kcol: 16 (over z_hi, y, core).
Axes of the slice: x: 4, y: 4, z: 8 (z_hi: 2, z_lo: 4; z = z_hi * 4 + z_lo), core: 2. Of those that a mesh axis runs over, the one named last changes fastest.
Arguments:
- queries: bfloat16 [1024, 8192], P(('qrow', 'kcol')), may hold values from -200 to 200
- keys_values: bfloat16 [2, 32768, 512], P(None, ('kcol', 'qrow')), may hold values from -8 to 8
- doc_blocks: int32 [256], replicated, may hold values from 0 to 11, never falling along the last dimension, each value on 1 to 129 neighbouring positions
Outputs:
- attended: bfloat16 [1024, 8192], P(('qrow', 'kcol'))
Inputs may be any that keep to these rules, and one draw needn't show every extreme that they name: doc_blocks[b] is the document of positions 128 b to 128 b + 127; each document covers 1 to 129 consecutive entries (blocks), one document exactly that many.
All inputs are finite; a program needn't handle non-finite values.
Results may differ from a plain program's by a relative error of at most 0.0046.
Values may be sent and summed in bfloat16 or wider, within the bound.
No kernel may reach another device: no remote copies, remote signals or barrier semaphores. Data moves between devices by JAX's collectives and lax.ppermute only.
A program may use at most 128 MiB of HBM per device.

v0:
```python
import math

import jax
import jax.numpy as jnp
from jax import lax
from jax.sharding import Mesh
from jax.sharding import PartitionSpec as P

QUERY_HEADS = 64
KEY_VALUE_HEADS = 4
HEAD_WIDTH = 128
QROW = ("qrow_0", "qrow_1")
QROW_KCOL = ("qrow_0", "qrow_1", "kcol")
KCOL_QROW = ("kcol", "qrow_0", "qrow_1")


masked_score = -1e30


def in_order(tiles, dim):
    tiles = jnp.moveaxis(tiles, 0, dim)
    lengths = tiles.shape
    return tiles.reshape(*lengths[:dim], lengths[dim] * lengths[dim + 1], *lengths[dim + 2 :])


def sent_to_all(value, axis):
    copies = jnp.broadcast_to(value, (lax.axis_size(axis), *value.shape))
    return lax.all_to_all(copies, axis, split_axis=0, concat_axis=0, tiled=True)


def gathered_copies(value, axis, dim):
    return in_order(sent_to_all(value, axis), dim)


def all_blocks(value, axes, sequence):
    tiles = value[None]
    for k in sequence:
        tiles = lax.all_gather(tiles, axes[k], axis=0, tiled=True)
    carried = [lax.axis_size(axes[k]) for k in reversed(sequence)]
    tiles = tiles.reshape(*carried, *value.shape)
    turned = sorted(range(len(sequence)), key=lambda place: sequence[len(sequence) - 1 - place])
    return tiles.transpose(*turned, *range(len(sequence), tiles.ndim)).reshape(-1, *value.shape)


def gathered_by_axis(value, axes, sequence, dim):
    return in_order(all_blocks(value, axes, sequence), dim)


def taken_together(value, axis):
    return sent_to_all(value, axis).max(axis=0)


def cut_along(value, dim, length):
    lengths = value.shape
    tiles = value.reshape(*lengths[:dim], length, lengths[dim] // length, *lengths[dim + 1 :])
    return jnp.moveaxis(tiles, dim, 0)


def summed_on_arrival(value, axis, dim):
    length = lax.axis_size(axis)
    tiles = lax.all_to_all(cut_along(value, dim, length), axis, 0, 0, tiled=True)
    return jnp.sum(tiles, axis=0)


def in_one_piece(arrays, axis, dim, along):
    widths = [a.shape[along] for a in arrays]
    both = jnp.concatenate(arrays, axis=along)
    out = summed_on_arrival(both, axis, dim)
    return tuple(jnp.split(out, [sum(widths[:k]) for k in range(1, len(widths))], axis=along))


def per_device(queries, keys_values, doc_blocks):
    local_rows = queries.shape[0]
    row_block = gathered_copies(queries, "kcol", 0)
    key_block = gathered_by_axis(keys_values, QROW, (0, 1), 1)
    block_rows = row_block.shape[0]
    range_keys = key_block.shape[1]
    total_queries = block_rows * lax.axis_size(QROW)
    total_keys = range_keys * lax.axis_size("kcol")
    stripe_len = total_keys * 128 // total_queries
    stripe_blocks = stripe_len // 128
    query_index = lax.axis_index(QROW) * block_rows + jnp.arange(block_rows, dtype=jnp.int32)
    query_pos = query_index // 128 * stripe_len + stripe_len - 128 + query_index % 128
    doc_slot = query_index // 128 * stripe_blocks + stripe_blocks - 1
    onehot = doc_slot[:, None] == jnp.arange(doc_blocks.shape[0], dtype=jnp.int32)[None, :]
    query_doc = jnp.sum(jnp.where(onehot, doc_blocks[None, :], 0), axis=1)
    key_first = lax.axis_index("kcol") * range_keys
    key_pos = key_first + jnp.arange(range_keys, dtype=jnp.int32)
    key_doc = jnp.repeat(
        lax.dynamic_slice_in_dim(doc_blocks, key_first // 128, range_keys // 128, 0), 128
    )
    live_mask = (query_doc[:, None] == key_doc[None, :]) & (key_pos[None, :] <= query_pos[:, None])
    query_group_width = QUERY_HEADS // KEY_VALUE_HEADS
    score_scale = 1.0 / math.sqrt(HEAD_WIDTH)
    out_list = []
    max_list = []
    sum_list = []
    for query_head_group in range(KEY_VALUE_HEADS):
        grouped = row_block[
            :,
            query_head_group
            * query_group_width
            * HEAD_WIDTH : (query_head_group + 1)
            * query_group_width
            * HEAD_WIDTH,
        ].reshape(block_rows, query_group_width, HEAD_WIDTH)
        key_part = key_block[
            0, :, query_head_group * HEAD_WIDTH : (query_head_group + 1) * HEAD_WIDTH
        ]
        value_part = key_block[
            1, :, query_head_group * HEAD_WIDTH : (query_head_group + 1) * HEAD_WIDTH
        ]
        scores = (
            jnp.einsum("qhd,kd->hqk", grouped, key_part, preferred_element_type=jnp.float32)
            * score_scale
        )
        scores = jnp.where(live_mask[None], scores, masked_score)
        row_max = jnp.max(scores, axis=2)
        weights = jnp.where(live_mask[None], jnp.exp(scores - row_max[:, :, None]), 0.0)
        row_sum = jnp.sum(weights, axis=2)
        partial_value = jnp.einsum(
            "hqk,kd->qhd",
            weights.astype(jnp.bfloat16),
            value_part,
            preferred_element_type=jnp.float32,
        )
        out_list.append(partial_value)
        max_list.append(row_max.T)
        sum_list.append(row_sum.T)
    part_out = jnp.concatenate(out_list, axis=1).reshape(block_rows, QUERY_HEADS * HEAD_WIDTH)
    part_max = jnp.concatenate(max_list, axis=1)
    part_sum = jnp.concatenate(sum_list, axis=1)
    global_max = taken_together(part_max, "kcol")
    factor = jnp.exp(part_max - global_max)
    rescaled = (part_out.reshape(block_rows, QUERY_HEADS, HEAD_WIDTH) * factor[:, :, None]).reshape(
        block_rows, QUERY_HEADS * HEAD_WIDTH
    )
    own_out, own_sum = in_one_piece((rescaled, part_sum * factor), "kcol", 0, 1)
    result = own_out.reshape(local_rows, QUERY_HEADS, HEAD_WIDTH) / own_sum[:, :, None]
    return result.reshape(local_rows, QUERY_HEADS * HEAD_WIDTH).astype(jnp.bfloat16)


def solution(mesh):
    split = Mesh(mesh.devices.reshape(4, 4, mesh.shape["kcol"]), ("qrow_0", "qrow_1", "kcol"))
    in_specs = (P(QROW_KCOL, None), P(None, KCOL_QROW, None), P())
    out_specs = P(QROW_KCOL, None)
    return jax.shard_map(
        per_device, mesh=split, in_specs=in_specs, out_specs=out_specs, check_vma=False
    )
```

profile of v0, /device:TPU:32, one launch (start us, length us, event | category | flops | bytes accessed | tf_op | source)
XLA Modules:
  0.0 246.5 jit_solution(8301358015825112225)
XLA Ops:
  6.5 0.7 all-gather.6.cloned.1.call-update
  7.3 36.0 %all-gather.6.cloned.1.call-done = bf16[8,128,512]{2,1,0:T(8,128)(2,1)} async-done(((bf16[2,128,512]{2,1,0:T(8,128)(2,1)}), bf16[8,128,512]{2,1,0:T(8,128)(2,1)}) %all-gather.6.cloned.1.call-update) | async-done | bytes 1048592 | tf_op jit(solution)/shard_map/all_gather | solution.py:38
  43.3 2.3 broadcast_in_dim.91
  45.6 8.5 %all-to-all-start = ((bf16[16,4,8192]{2,1,0:T(4,128)(2,1)}), bf16[16,4,8192]{2,1,0:T(4,128)(2,1)S(1)}, u32[]{:S(2)}, u32[]{:S(2)}) async-start(bf16[16,4,8192]{2,1,0:T(4,128)(2,1)} %broadcast_in_dim.91), calls=%async_computation | async-start | bytes 2097152 | tf_op jit(solution)/shard_map/all_to_all | solution.py:28
  54.2 0.8 dynamic_slice.3
  55.0 0.9 select_reduce_fusion
  56.1 29.3 %all-to-all-done = bf16[16,4,8192]{2,1,0:T(4,128)(2,1)S(1)} async-done(((bf16[16,4,8192]{2,1,0:T(4,128)(2,1)}), bf16[16,4,8192]{2,1,0:T(4,128)(2,1)S(1)}, u32[]{:S(2)}, u32[]{:S(2)}) %all-to-all-start) | async-done | bytes 1048608 | tf_op jit(solution)/shard_map/all_to_all | solution.py:28
  85.3 0.3 reshape.185
  85.7 11.3 %all-gather.4.cloned.1.call-done = bf16[16,2,128,512]{3,2,1,0:T(8,128)(2,1)} async-done(((bf16[4,2,128,512]{3,2,1,0:T(8,128)(2,1)}), bf16[16,2,128,512]{3,2,1,0:T(8,128)(2,1)}) %all-gather.4.cloned.1.call-update) | async-done | bytes 4194320 | tf_op jit(solution)/shard_map/all_gather | solution.py:38
  97.0 2.6 %copy.34 = bf16[4,4,2,128,512]{4,3,1,0,2:T(8,128)(2,1)S(1)} copy(bf16[4,4,2,128,512]{4,3,2,0,1:T(8,128)(2,1)} %bitcast.164) | data formatting | bytes 8388608 | tf_op jit(solution)/shard_map/transpose | solution.py:42
  99.6 4.5 %fusion.36 = f32[2048,64,16]{0,1,2:T(8,128)} fusion(bf16[2,2048,512]{2,1,0:T(8,128)(2,1)S(1)} %bitcast.156, bf16[8,16,8,128]{3,2,1,0:T(8,128)(2,1)S(1)} %get-tuple-element.12), kind=kOutput, calls=%fused_computation.36 | convolution fusion | flops 536870912 | bytes 9175040 | tf_op jit(solution)/shard_map/qhd,kd->hqk/dot_general | solution.py:114
  104.1 4.5 %fusion.37 = f32[2048,64,16]{0,1,2:T(8,128)} fusion(bf16[2,2048,512]{2,1,0:T(8,128)(2,1)S(1)} %bitcast.157, bf16[8,16,8,128]{3,2,1,0:T(8,128)(2,1)S(1)} %get-tuple-element.13), kind=kOutput, calls=%fused_computation.39 | convolution fusion | flops 536870912 | bytes 9175040 | tf_op jit(solution)/shard_map/qhd,kd->hqk/dot_general | solution.py:114
  108.6 4.7 %fusion = (f32[16,64]{1,0:T(8,128)S(1)}, f32[2048,64,16]{0,1,2:T(8,128)}) fusion(pred[64,2048]{1,0:T(8,128)(4,1)S(1)} %compare_and_fusion, bf16[8,16,8,128]{3,2,1,0:T(8,128)(2,1)S(1)} %get-tuple-element.15, bf16[2,2048,512]{2,1,0:T(8,128)(2,1)S(1)} %bitcast.158), kind=kOutput, calls=%fused_computation.8 | convolution fusion | flops 543161344 | bytes 9310208 | tf_op jit(solution)/shard_map/qhd,kd->hqk/dot_general | solution.py:114
  113.4 4.9 %fusion.24 = f32[64,16,128]{2,0,1:T(8,128)S(1)} fusion(f32[2048,64,16]{0,1,2:T(8,128)} %get-tuple-element.17, f32[16,64]{1,0:T(8,128)S(1)} %get-tuple-element.16, pred[64,2048]{1,0:T(8,128)(4,1)S(1)} %compare_and_fusion, bf16[2,2048,512]{2,1,0:T(8,128)(2,1)} %bitcast.159), kind=kOutput, calls=%fused_computation.30 | convolution fusion | flops 547356672 | bytes 9572352 | tf_op jit(solution)/shard_map/hqk,kd->qhd/dot_general | solution.py:121
  118.3 1.1 copy-done
  119.4 12.1 %fusion.4 = (f32[16,64]{1,0:T(8,128)S(1)}, f32[16,64]{1,0:T(8,128)S(1)}, f32[16,64]{1,0:T(8,128)S(1)}, f32[16,64]{1,0:T(8,128)S(1)}, f32[2048,64,16]{0,1,2:T(8,128)}) fusion(f32[2048,64,16]{0,1,2:T(8,128)} %get-tuple-element.17, f32[16,64]{1,0:T(8,128)S(1)} %get-tuple-element.16, pred[64,2048]{1,0:T(8,128)(4,1)S(1)} %compare_and_fusion, ...), kind=kOutput, calls=%fused_computation.12 | convolution fusion | flops 566226944 | bytes 34492416 | tf_op jit(solution)/shard_map/qhd,kd->hqk/dot_general | solution.py:114
  131.5 3.2 %fusion.33 = f32[64,16,128]{2,0,1:T(8,128)S(1)} fusion(f32[2048,64,16]{0,1,2:T(8,128)S(1)} %bitcast.155, f32[16,64]{1,0:T(8,128)S(1)} %get-tuple-element.8, pred[64,2048]{1,0:T(8,128)(4,1)S(1)} %compare_and_fusion, bf16[2,2048,512]{2,1,0:T(8,128)(2,1)} %bitcast.161), kind=kOutput, calls=%fused_computation.33 | convolution fusion | flops 547356672 | bytes 9572352 | tf_op jit(solution)/shard_map/hqk,kd->qhd/dot_general | solution.py:121
  134.7 3.2 %fusion.30 = f32[64,16,128]{2,0,1:T(8,128)S(1)} fusion(f32[2048,64,16]{0,1,2:T(8,128)S(1)} %copy-done, f32[16,64]{1,0:T(8,128)S(1)} %get-tuple-element.7, pred[64,2048]{1,0:T(8,128)(4,1)S(1)} %compare_and_fusion, bf16[2,2048,512]{2,1,0:T(8,128)(2,1)} %bitcast.162), kind=kOutput, calls=%fused_computation.32 | convolution fusion | flops 547356672 | bytes 9572352 | tf_op jit(solution)/shard_map/hqk,kd->qhd/dot_general | solution.py:121
  138.2 12.1 %fusion.6 = (f32[16,64]{1,0:T(8,128)S(1)}, f32[16,64]{1,0:T(8,128)S(1)}, f32[16,64]{1,0:T(8,128)S(1)}) fusion(f32[2048,64,16]{0,1,2:T(8,128)} %get-tuple-element.18, f32[16,64]{1,0:T(8,128)S(1)} %get-tuple-element.6, pred[64,2048]{1,0:T(8,128)(4,1)S(1)} %compare_and_fusion, f32[16,64]{1,0:T(8,128)S(1)} %get-tuple-element.7, f32[2048,64,16]{0,1,2:T(8,128)} %fusion.37, ...), kind=kLoop, calls=%fused_computation.14 | loop fusion | flops 31454208 | bytes 25321472 | tf_op jit(solution)/shard_map/reduce_sum | solution.py:120
  150.7 1.0 reshape.199
  151.8 8.7 %all-to-all-start.1 = ((f32[16,1,4096]{2,1,0:T(1,128)}), f32[16,1,4096]{2,1,0:T(1,128)S(1)}, u32[]{:S(2)}, u32[]{:S(2)}) async-start(f32[16,1,4096]{2,1,0:T(1,128)} %reshape.199), calls=%async_computation.1 | async-start | bytes 524288 | tf_op jit(solution)/shard_map/all_to_all | solution.py:28
  160.4 4.7 %fusion.27 = f32[64,16,128]{2,0,1:T(8,128)S(1)} fusion(f32[2048,64,16]{0,1,2:T(8,128)} %get-tuple-element.18, f32[16,64]{1,0:T(8,128)S(1)} %get-tuple-element.6, pred[64,2048]{1,0:T(8,128)(4,1)S(1)} %compare_and_fusion, bf16[2,2048,512]{2,1,0:T(8,128)(2,1)} %bitcast.163), kind=kOutput, calls=%fused_computation.31 | convolution fusion | flops 547356672 | bytes 9572352 | tf_op jit(solution)/shard_map/hqk,kd->qhd/dot_general | solution.py:121
  165.2 10.0 %all-to-all-done.1 = f32[16,1,4096]{2,1,0:T(1,128)S(1)} async-done(((f32[16,1,4096]{2,1,0:T(1,128)}), f32[16,1,4096]{2,1,0:T(1,128)S(1)}, u32[]{:S(2)}, u32[]{:S(2)}) %all-to-all-start.1) | async-done | bytes 262176 | tf_op jit(solution)/shard_map/all_to_all | solution.py:28
  175.2 0.5 broadcast.220
  175.7 1.3 reduce
  177.4 0.7 maximum_multiply_fusion
  178.1 2.6 %copy.41 = f32[64,64,128]{2,1,0:T(8,128)} copy(f32[64,64,128]{2,0,1:T(8,128)S(1)} %maximum_multiply_fusion) | data formatting | bytes 4194304 | tf_op jit(solution)/shard_map/mul | solution.py:135
  180.7 2.1 mul.79
  183.0 0.5 pad_maximum_fusion
  183.5 55.0 %all_to_all.15 = f32[16,4,8256]{2,1,0:T(4,128)S(1)} all-to-all(f32[16,4,8256]{2,1,0:T(4,128)S(1)} %pad_maximum_fusion), channel_id=1, replica_groups=mesh['qrow_0'=4,'qrow_1'=4,'kcol'=16] {'kcol'}, dimensions={0} | all-to-all | bytes 4227072 | tf_op jit(solution)/shard_map/all_to_all | solution.py:61
  238.4 0.4 reduce_sum.59
  238.9 0.7 fusion.48
  (35 shorter events, 1.9 us)
Async XLA Ops:
  6.5 36.8 %all-gather.6.cloned.1.call-start = ((), (), s32[]{:S(2)}) async-start(), calls=%async_computation.4 | async-start | bytes 1310720 | tf_op jit(solution)/shard_map/all_gather | solution.py:38
  7.3 89.7 %all-gather.4.cloned.1.call-start = ((), (), s32[]{:S(2)}) async-start(), calls=%async_computation.3 | async-start | bytes 5242880 | tf_op jit(solution)/shard_map/all_gather | solution.py:38
  45.6 39.7 %all-to-all-start = ((bf16[16,4,8192]{2,1,0:T(4,128)(2,1)}), bf16[16,4,8192]{2,1,0:T(4,128)(2,1)S(1)}, u32[]{:S(2)}, u32[]{:S(2)}) async-start(bf16[16,4,8192]{2,1,0:T(4,128)(2,1)} %broadcast_in_dim.91), calls=%async_computation | async-start | bytes 2097152 | tf_op jit(solution)/shard_map/all_to_all | solution.py:28
  99.6 8.9 %copy-start.1 = (bf16[4,4,2,128,512]{4,3,1,0,2:T(8,128)(2,1)}, bf16[4,4,2,128,512]{4,3,1,0,2:T(8,128)(2,1)S(1)}, u32[]{:S(2)}) copy-start(bf16[4,4,2,128,512]{4,3,1,0,2:T(8,128)(2,1)S(1)} %copy.34) | copy-start | bytes 12582916
  113.4 6.0 %copy-start = (f32[2048,64,16]{0,1,2:T(8,128)S(1)}, f32[2048,64,16]{0,1,2:T(8,128)}, u32[]{:S(2)}) copy-start(f32[2048,64,16]{0,1,2:T(8,128)} %fusion.37) | copy-start | bytes 25165828
  113.4 18.1 %slice-start = ((s8[8388608]{0:T(1024)(128)(4,1)}), s8[4194304]{0:T(1024)(128)(4,1)S(1)}, s32[]{:S(2)}) async-start(s8[8388608]{0:T(1024)(128)(4,1)} %bitcast.154), calls=%async_computation.5 | async-start | bytes 8388608
  119.4 12.1 %slice-start.1 = ((s8[8388608]{0:T(1024)(128)(4,1)}), s8[4194304]{0:T(1024)(128)(4,1)S(1)}, s32[]{:S(2)}) async-start(s8[8388608]{0:T(1024)(128)(4,1)} %bitcast.154), calls=%async_computation.6 | async-start | bytes 8388608
  151.8 23.4 %all-to-all-start.1 = ((f32[16,1,4096]{2,1,0:T(1,128)}), f32[16,1,4096]{2,1,0:T(1,128)S(1)}, u32[]{:S(2)}, u32[]{:S(2)}) async-start(f32[16,1,4096]{2,1,0:T(1,128)} %reshape.199), calls=%async_computation.1 | async-start | bytes 524288 | tf_op jit(solution)/shard_map/all_to_all | solution.py:28
Sparse Core Ops, SparseCore 0:
  9.2 34.1 all-gather.5
  45.1 51.8 all-gather.3
where the time goes:
time: 248 us; the launch traced here: 246 us
  waiting for transfers between devices  87.3 us (35%)
  blocking collectives  55 us (22%)
  matrix products  41.7 us (17%)
  starting transfers between devices  17.2 us (7%)
  other arithmetic  17.1 us (7%)
  local copies, waits for them, and re-layouts  14.6 us (6%)
  between operations  13.6 us (5%)
    all_to_all x1, blocking collectives, summed_on_arrival(): lax.all_to_all(cut_along(value, dim, length), axis, 0, 0, tiled=True)  55 us
    all_gather x2, waiting for transfers between devices, all_blocks(): tiles = lax.all_gather(tiles, axes[k], axis=0, tiled=True)  47.3 us
    all_to_all x2, waiting for transfers between devices, sent_to_all(): return lax.all_to_all(copies, axis, split_axis=0, concat_axis=0, tiled=True)  39.3 us
    dot_general x4, matrix products, per_device(): jnp.einsum('qhd,kd->hqk', grouped, key_part, preferred_element_type=jnp.f...  25.8 us
    all_to_all x2, starting transfers between devices, sent_to_all(): return lax.all_to_all(copies, axis, split_axis=0, concat_axis=0, tiled=True)  17.2 us
    dot_general x4, matrix products, per_device(): jnp.einsum('hqk,kd->qhd', weights.astype(jnp.bfloat16), value_part, prefe...  15.9 us
    reduce_sum x1, other arithmetic, per_device(): row_sum = jnp.sum(weights, axis=2)  12.1 us
  transfers between devices with their start and end apart: 4, of which 4 were waited for; matrix products, arithmetic and copies ran while one was open for 4% of the time, Pallas kernels for 0%

commit v1 on v0

v1 whole, which is shorter than its diff:
```python
import functools
import math

import jax
import jax.numpy as jnp
from jax import lax
from jax.experimental import pallas as pl
from jax.experimental.pallas import tpu as pltpu
from jax.sharding import Mesh
from jax.sharding import PartitionSpec as P

HEADS = 64
GROUPS = 4
WIDTH = 128
BLOCK = 128
HEADS_PER_GROUP = HEADS // GROUPS
MASKED = -1e30
EXP_SCALE = math.log2(math.e) / math.sqrt(WIDTH)
SLOT_ROWS = 80
VMEM = pl.BlockSpec(memory_space=pltpu.VMEM)
SMEM = pl.BlockSpec(memory_space=pltpu.SMEM)


def three_pieces(value):
    hi = value.astype(jnp.bfloat16).astype(jnp.float32)
    rest = value - hi
    mid = rest.astype(jnp.bfloat16).astype(jnp.float32)
    return hi, mid, rest - mid


def attend(scal, q_ref, a0, a1, a2, a3, b0, b1, out_ref, s_scr, p_scr, acc, m_scr, l_scr):
    zl, x, core, x0 = scal[8], scal[9], scal[10], scal[11]
    own = (a0, a1, a2, a3)

    def block(crel, xr, s, which):
        if crel == 0:
            return own[xr][s, which]
        half = b0 if xr < 2 else b1
        return half[(xr % 2) * 4 + s, which]

    for group in range(4):
        lo, hi, diagonal = scal[group], scal[4 + group], scal[12 + group]
        rows = pl.ds(group * 512, 512)

        @pl.when(lo < hi)
        def _():
            m_scr[...] = jnp.full_like(m_scr, MASKED)
            l_scr[...] = jnp.zeros_like(l_scr)
            acc[...] = jnp.zeros_like(acc)
            for crel in range(2):
                c_at = core ^ crel
                first = jnp.clip(lo - 16 * c_at, 0, 16)
                last = jnp.clip(hi - 16 * c_at, 0, 16)

                def chunk(zl_at, carry, crel=crel, c_at=c_at):
                    s = zl_at ^ zl
                    keys = jnp.concatenate([block(crel, xr, s, 0) for xr in range(4)], axis=0)
                    s_scr[...] = lax.dot_general(
                        keys,
                        q_ref[rows, :],
                        (((1,), (1,)), ((), ())),
                        preferred_element_type=jnp.float32,
                    )
                    base = c_at * 16 + zl_at * 4

                    @pl.when((diagonal >= base) & (diagonal < base + 4))
                    def _():
                        at = pl.ds(pl.multiple_of(((diagonal - base - x) & 3) * 128, 128), 128)
                        key = lax.broadcasted_iota(jnp.int32, (128, 512), 0)
                        row = lax.broadcasted_iota(jnp.int32, (128, 512), 1)
                        query = x0 * 64 + (row >> 6) * 8 + core * 4 + (row & 3)
                        s_scr[at, :] = jnp.where(key <= query, s_scr[at, :], MASKED)

                    m_old = m_scr[0:1, :]
                    m_new = m_old
                    bias = []
                    for xr in range(4):
                        at = base + ((x + xr) & 3)
                        dead = (at < lo) | (at >= hi)
                        bias.append(jnp.where(dead, jnp.float32(MASKED), jnp.float32(0.0)))
                        top = jnp.max(s_scr[xr * 128 : (xr + 1) * 128, :], axis=0, keepdims=True)
                        m_new = jnp.maximum(m_new, top + bias[xr])
                    total = jnp.zeros((1, 512), jnp.float32)
                    for xr in range(4):
                        at = slice(xr * 128, (xr + 1) * 128)
                        p = jnp.exp2((s_scr[at, :] - (m_new - bias[xr])) * EXP_SCALE)
                        total = total + jnp.sum(p, axis=0, keepdims=True)
                        p_scr[at, :] = p.astype(jnp.bfloat16)
                    alpha = jnp.exp2((m_old - m_new) * EXP_SCALE)
                    m_scr[0:1, :] = m_new
                    l_scr[0:1, :] = l_scr[0:1, :] * alpha + total
                    values = jnp.concatenate([block(crel, xr, s, 1) for xr in range(4)], axis=0)
                    acc[...] = acc[...] * alpha + lax.dot_general(
                        values,
                        p_scr[...],
                        (((0,), (0,)), ((), ())),
                        preferred_element_type=jnp.float32,
                    )
                    return carry

                lax.fori_loop(first // 4, (last + 3) // 4, chunk, 0)
            part = acc[...].T.astype(jnp.bfloat16)
            stats = (*three_pieces(m_scr[0:1, :]), *three_pieces(l_scr[0:1, :]))
            stats = jnp.concatenate([*stats, jnp.zeros((10, 512), jnp.float32)], axis=0)
            stats = stats.astype(jnp.bfloat16)
            for j in range(8):
                out_ref[group * 8 + j, 0:64, :] = part[j * 64 : (j + 1) * 64]
                out_ref[group * 8 + j, 64:80, :] = stats[:, (j // 2) * 128 : (j // 2 + 1) * 128]

        @pl.when(lo >= hi)
        def _():
            row = lax.broadcasted_iota(jnp.int32, (16, 128), 0)
            stats = jnp.where(row == 0, jnp.float32(MASKED), jnp.float32(0.0)).astype(jnp.bfloat16)
            for j in range(8):
                out_ref[group * 8 + j, 0:64, :] = jnp.zeros((64, 128), jnp.bfloat16)
                out_ref[group * 8 + j, 64:80, :] = stats


def combine(scal, parts, out_ref):
    odd = scal[16] & 1
    for g in range(GROUPS):
        m, l = [], []
        for plane in range(8):
            st = parts[g * 8 + plane, 64:80, :].astype(jnp.float32)
            m.append(st[0:1] + st[1:2] + st[2:3])
            l.append(st[3:4] + st[4:5] + st[5:6])
        m, l = jnp.concatenate(m, axis=0), jnp.concatenate(l, axis=0)
        w = jnp.exp2((m - jnp.max(m, axis=0, keepdims=True)) * EXP_SCALE)
        w = w / jnp.sum(w * l, axis=0, keepdims=True)
        w = jnp.where(odd == 1, pltpu.roll(w, 64, 1), w)
        w = w.T
        total = jnp.zeros((64, 128), jnp.float32)
        for plane in range(8):
            part = parts[g * 8 + plane, 0:64, :].astype(jnp.float32)
            total = total + part * w[0:64, plane : plane + 1]
        for h in range(HEADS_PER_GROUP):
            at = (g * HEADS_PER_GROUP + h) * WIDTH
            out_ref[:, at : at + WIDTH] = total[h * 4 : (h + 1) * 4, :].astype(jnp.bfloat16)


def from_x(k):
    return [((i + k) % 4, i) for i in range(4)]


def per_device(queries, keys_values, doc_blocks):
    zl, x, zh, y, core = (lax.axis_index(a) for a in ("zl", "x", "zh", "y", "core"))
    planes = ("zl", "zh", "y")
    q = queries.reshape(4, GROUPS, HEADS_PER_GROUP, WIDTH).transpose(1, 2, 0, 3)
    q = q.reshape(GROUPS, 1, 64, WIDTH)
    q = jnp.broadcast_to(q, (GROUPS, 8, 64, WIDTH)).reshape(32, 64, WIDTH)
    q = lax.all_to_all(q, planes, 0, 0, tiled=True).reshape(2048, WIDTH)
    heads = keys_values.reshape(2, BLOCK, GROUPS, WIDTH).transpose(2, 0, 1, 3)
    pieces = [lax.dynamic_index_in_dim(heads, zl, 0, False)]
    for s in (1, 2, 3):
        piece = lax.dynamic_index_in_dim(heads, zl ^ s, 0, False)
        pieces.append(lax.ppermute(piece, "zl", [(i, i ^ s) for i in range(4)]))
    a0 = jnp.stack(pieces)
    a1, a2, a3 = (lax.ppermute(a0, "x", from_x(k)) for k in (1, 2, 3))
    swap = [(0, 1), (1, 0)]
    b0 = lax.ppermute(jnp.concatenate([a0, a1]), "core", swap)
    b1 = lax.ppermute(jnp.concatenate([a2, a3]), "core", swap)
    plane = zh * 4 + y
    query_block = 2 * jnp.arange(4, dtype=jnp.int32) + x // 2
    at = query_block * 32 + 31
    index = jnp.arange(256, dtype=jnp.int32)
    own_doc = jnp.sum(jnp.where(index[None] == at[:, None], doc_blocks[None], 0), axis=1)
    start = jnp.sum((doc_blocks[None] < own_doc[:, None]).astype(jnp.int32), axis=1)
    lo = jnp.clip(start - 32 * plane, 0, 32)
    hi = jnp.clip(at + 1 - 32 * plane, 0, 32)
    diagonal = at - 32 * plane
    mine = jnp.stack([zl, x, core, x % 2]).astype(jnp.int32)
    scal = jnp.concatenate([lo, hi, mine, diagonal, (zh * 4 + y)[None]]).astype(jnp.int32)

    part = pl.pallas_call(
        attend,
        out_shape=jax.ShapeDtypeStruct((32, SLOT_ROWS, WIDTH), jnp.bfloat16),
        in_specs=[SMEM] + [VMEM] * 7,
        out_specs=VMEM,
        scratch_shapes=[
            pltpu.VMEM((512, 512), jnp.float32),
            pltpu.VMEM((512, 512), jnp.bfloat16),
            pltpu.VMEM((WIDTH, 512), jnp.float32),
            pltpu.VMEM((8, 512), jnp.float32),
            pltpu.VMEM((8, 512), jnp.float32),
        ],
        compiler_params=pltpu.CompilerParams(vmem_limit_bytes=32 * 1024 * 1024),
        name="attend",
    )(scal, q, a0, a1, a2, a3, b0, b1)
    part = lax.all_to_all(part, planes, 0, 0, tiled=True)
    return pl.pallas_call(
        combine,
        out_shape=jax.ShapeDtypeStruct((4, HEADS * WIDTH), jnp.bfloat16),
        in_specs=[SMEM, VMEM],
        out_specs=VMEM,
        compiler_params=pltpu.CompilerParams(vmem_limit_bytes=32 * 1024 * 1024),
        name="combine",
    )(scal, part)


def solution(mesh):
    split = Mesh(mesh.devices.reshape(4, 4, 2, 4, 2), ("zl", "x", "zh", "y", "core"))
    in_specs = (
        P(("zl", "x", "zh", "y", "core"), None),
        P(None, ("zh", "y", "core", "zl", "x"), None),
        P(),
    )
    out_specs = P(("zl", "x", "zh", "y", "core"), None)
    return jax.shard_map(
        per_device, mesh=split, in_specs=in_specs, out_specs=out_specs, check_vma=False
    )
```

time: 248 us -> 80.1 us (0.32)
  the two profiles are of different devices: /device:TPU:32 before, /device:TPU:4 now
where the time goes in v1:
time: 80.1 us; the launch traced here: 79.5 us
  blocking collectives  40 us (50%)
  starting transfers between devices  19.3 us (24%)
  waiting for transfers between devices  10.2 us (13%)
  local copies, waits for them, and re-layouts  6.66 us (8%)
  Pallas kernels  2.81 us (4%)
    all_to_all x1, blocking collectives, per_device(): part = lax.all_to_all(part, planes, 0, 0, tiled=True)  40 us
    all_to_all x1, starting transfers between devices, per_device(): q = lax.all_to_all(q, planes, 0, 0, tiled=True).reshape(2048, WIDTH)  10.5 us
    ppermute x3, waiting for transfers between devices, per_device(): a1, a2, a3 = (lax.ppermute(a0, 'x', from_x(k)) for k in (1, 2, 3))  9.22 us
    ppermute x3, starting transfers between devices, per_device(): pieces.append(lax.ppermute(piece, 'zl', [(i, i ^ s) for i in range(4)]))  5.44 us
    unnamed x11, local copies, waits for them, and re-layouts  3.39 us
    ppermute x3, starting transfers between devices, per_device(): a1, a2, a3 = (lax.ppermute(a0, 'x', from_x(k)) for k in (1, 2, 3))  3.21 us
    pallas_call x1, Pallas kernels, per_device(): pl.pallas_call(combine, out_shape=jax.ShapeDtypeStruct((4, HEADS * WIDTH)...  2.15 us
  transfers between devices with their start and end apart: 9, of which 4 were waited for; matrix products, arithmetic and copies ran while one was open for 6% of the time, Pallas kernels for 0%

profile of v1, /device:TPU:4, one launch (start us, length us, event | category | flops | bytes accessed | tf_op | source)
XLA Modules:
  0.0 79.5 jit_solution(17957993076527071393)
XLA Ops:
  0.0 1.0 %reshape.33 = bf16[2,128,4,128]{3,2,1,0:T(4,128)(2,1)S(1)} reshape(bf16[2,128,512]{2,1,0:T(8,128)(2,1)} %param.4) | data formatting | bytes 524288 | tf_op jit(solution)/shard_map/reshape | solution.py:152
  1.0 0.6 constant_dynamic-slice_fusion.2
  1.6 4.7 %collective-permute-start.2 = (bf16[2,128,128]{2,1,0:T(8,128)(2,1)S(1)}, bf16[2,128,128]{2,1,0:T(8,128)(2,1)S(1)}, u32[]{:S(2)}, u32[]{:S(2)}) collective-permute-start(bf16[2,128,128]{2,1,0:T(8,128)(2,1)S(1)} %bitcast.35), channel_id=1, source_target_pairs={{0,192},{64,128},{128,64},{192,0},{1,193},{65,129},{129,65},{193,1... | collective-permute-start | bytes 196616 | tf_op jit(solution)/shard_map/ppermute | solution.py:156
  6.3 0.1 collective-permute-start
  6.4 0.0 copy-start
  6.5 0.6 collective-permute-start.1
  7.1 0.2 copy-done
  7.3 0.9 %broadcast_in_dim.28 = bf16[4,8,64,128]{3,2,1,0:T(8,128)(2,1)} broadcast(bf16[4,64,128]{2,1,0:T(8,128)(2,1)S(1)} %bitcast.34), dimensions={0,2,3} | broadcast | bytes 589824 | tf_op jit(solution)/shard_map/broadcast_in_dim | solution.py:150
  8.2 10.5 %all-to-all-start = ((bf16[32,64,128]{2,1,0:T(8,128)(2,1)}), bf16[32,64,128]{2,1,0:T(8,128)(2,1)S(1)}, u32[]{:S(2)}, u32[]{:S(2)}) async-start(bf16[32,64,128]{2,1,0:T(8,128)(2,1)} %bitcast.8), calls=%async_computation | async-start | bytes 1048576 | tf_op jit(solution)/shard_map/all_to_all | solution.py:151
  18.7 0.6 constant_dynamic-update-slice_fusion.4
  19.4 0.0 collective-permute-done.2
  19.4 0.0 collective-permute-done
  19.4 0.0 collective-permute-done.1
  19.4 1.3 %collective-permute-start.5 = (bf16[4,2,128,128]{3,2,1,0:T(8,128)(2,1)S(1)}, bf16[4,2,128,128]{3,2,1,0:T(8,128)(2,1)S(1)}, u32[]{:S(2)}, u32[]{:S(2)}) collective-permute-start(bf16[4,2,128,128]{3,2,1,0:T(8,128)(2,1)S(1)} %pad_maximum_fusion.1.a0), channel_id=1, source_target_pairs={{48,0},{0,16},{16,32},{32,48},{49,1},{1,17},{17,33},{33,49},{50,2}... | collective-permute-start | bytes 786440 | tf_op jit(solution)/shard_map/ppermute | solution.py:158
  20.7 0.8 %collective-permute-start.4 = (bf16[4,2,128,128]{3,2,1,0:T(8,128)(2,1)S(1)}, bf16[4,2,128,128]{3,2,1,0:T(8,128)(2,1)S(1)}, u32[]{:S(2)}, u32[]{:S(2)}) collective-permute-start(bf16[4,2,128,128]{3,2,1,0:T(8,128)(2,1)S(1)} %pad_maximum_fusion.1.a0), channel_id=1, source_target_pairs={{32,0},{48,16},{0,32},{16,48},{33,1},{49,17},{1,33},{17,49},{34,2}... | collective-permute-start | bytes 786440 | tf_op jit(solution)/shard_map/ppermute | solution.py:158
  21.5 1.1 %collective-permute-start.3 = (bf16[4,2,128,128]{3,2,1,0:T(8,128)(2,1)S(1)}, bf16[4,2,128,128]{3,2,1,0:T(8,128)(2,1)S(1)}, u32[]{:S(2)}, u32[]{:S(2)}) collective-permute-start(bf16[4,2,128,128]{3,2,1,0:T(8,128)(2,1)S(1)} %pad_maximum_fusion.1.a0), channel_id=1, source_target_pairs={{16,0},{32,16},{48,32},{0,48},{17,1},{33,17},{49,33},{1,49},{18,2}... | collective-permute-start | bytes 786440 | tf_op jit(solution)/shard_map/ppermute | solution.py:158
  22.7 0.6 constant_dynamic-update-slice_fusion.3
  23.3 0.6 constant_dynamic-update-slice_fusion.2
  23.9 0.6 constant_dynamic-update-slice_fusion.1
  24.5 4.3 %collective-permute-done.5.a3 = bf16[4,2,128,128]{3,2,1,0:T(8,128)(2,1)S(1)} collective-permute-done((bf16[4,2,128,128]{3,2,1,0:T(8,128)(2,1)S(1)}, bf16[4,2,128,128]{3,2,1,0:T(8,128)(2,1)S(1)}, u32[]{:S(2)}, u32[]{:S(2)}) %collective-permute-start.5) | collective-permute-done | bytes 262176 | tf_op jit(solution)/shard_map/ppermute | solution.py:158
  28.8 3.3 %collective-permute-done.4.a2 = bf16[4,2,128,128]{3,2,1,0:T(8,128)(2,1)S(1)} collective-permute-done((bf16[4,2,128,128]{3,2,1,0:T(8,128)(2,1)S(1)}, bf16[4,2,128,128]{3,2,1,0:T(8,128)(2,1)S(1)}, u32[]{:S(2)}, u32[]{:S(2)}) %collective-permute-start.4) | collective-permute-done | bytes 262176 | tf_op jit(solution)/shard_map/ppermute | solution.py:158
  32.1 0.1 collective-permute-start.7
  32.2 1.7 %collective-permute-done.3.a1 = bf16[4,2,128,128]{3,2,1,0:T(8,128)(2,1)S(1)} collective-permute-done((bf16[4,2,128,128]{3,2,1,0:T(8,128)(2,1)S(1)}, bf16[4,2,128,128]{3,2,1,0:T(8,128)(2,1)S(1)}, u32[]{:S(2)}, u32[]{:S(2)}) %collective-permute-start.3) | collective-permute-done | bytes 262176 | tf_op jit(solution)/shard_map/ppermute | solution.py:158
  33.9 0.7 constant_dynamic-update-slice_fusion
  34.6 0.7 copy-done.1
  35.3 0.2 select_reduce_fusion
  35.5 0.2 convert_reduce_fusion
  35.7 0.1 concatenate.10.scal
  35.8 1.0 %collective-permute-done.6.b0 = bf16[8,2,128,128]{3,2,1,0:T(8,128)(2,1)S(1)} collective-permute-done((bf16[8,2,128,128]{3,2,1,0:T(8,128)(2,1)}, bf16[8,2,128,128]{3,2,1,0:T(8,128)(2,1)S(1)}, u32[]{:S(2)}, u32[]{:S(2)}) %collective-permute-start.6) | collective-permute-done | bytes 524320 | tf_op jit(solution)/shard_map/ppermute | solution.py:160
  36.7 0.7 attend.1
  37.4 40.0 %all_to_all.10.parts = bf16[32,80,128]{2,1,0:T(8,128)(2,1)S(1)} all-to-all(bf16[32,80,128]{2,1,0:T(8,128)(2,1)S(1)} %attend.1), channel_id=1, replica_groups=mesh['zl'=4,'x'=4,'zh'=2,'y'=4,'core'=2] {'zl','zh','y'}, dimensions={0} | all-to-all | bytes 1310720 | tf_op jit(solution)/shard_map/all_to_all | solution.py:189
  77.4 2.1 %combine.1 = bf16[4,8192]{1,0:T(4,128)(2,1)} custom-call(s32[17]{0:T(128)S(1)} %concatenate.10.scal, bf16[32,80,128]{2,1,0:T(8,128)(2,1)S(1)} %all_to_all.10.parts), custom_call_target="tpu_custom_call" | custom-call | tf_op jit(solution)/shard_map/combine/pallas_call | solution.py:190
  (12 shorter events, 0.2 us)
Async XLA Ops:
  1.6 17.8 %collective-permute-start.2 = (bf16[2,128,128]{2,1,0:T(8,128)(2,1)S(1)}, bf16[2,128,128]{2,1,0:T(8,128)(2,1)S(1)}, u32[]{:S(2)}, u32[]{:S(2)}) collective-permute-start(bf16[2,128,128]{2,1,0:T(8,128)(2,1)S(1)} %bitcast.35), channel_id=1, source_target_pairs={{0,192},{64,128},{128,64},{192,0},{1,193},{65,129},{129,65},{193,1... | collective-permute-start | bytes 196616 | tf_op jit(solution)/shard_map/ppermute | solution.py:156
  6.3 13.0 %collective-permute-start = (bf16[2,128,128]{2,1,0:T(8,128)(2,1)S(1)}, bf16[2,128,128]{2,1,0:T(8,128)(2,1)S(1)}, u32[]{:S(2)}, u32[]{:S(2)}) collective-permute-start(bf16[2,128,128]{2,1,0:T(8,128)(2,1)S(1)} %bitcast.36), channel_id=1, source_target_pairs={{0,64},{64,0},{128,192},{192,128},{1,65},{65,1},{129,193},{193,129... | collective-permute-start | bytes 196616 | tf_op jit(solution)/shard_map/ppermute | solution.py:156
  6.4 0.8 %copy-start = (bf16[4,8192]{1,0:T(4,128)(2,1)S(1)}, bf16[4,8192]{1,0:T(4,128)(2,1)}, u32[]{:S(2)}) copy-start(bf16[4,8192]{1,0:T(4,128)(2,1)} %param.3) | copy-start | bytes 196612
  6.5 12.9 %collective-permute-start.1 = (bf16[2,128,128]{2,1,0:T(8,128)(2,1)S(1)}, bf16[2,128,128]{2,1,0:T(8,128)(2,1)S(1)}, u32[]{:S(2)}, u32[]{:S(2)}) collective-permute-start(bf16[2,128,128]{2,1,0:T(8,128)(2,1)S(1)} %bitcast.37), channel_id=1, source_target_pairs={{0,128},{64,192},{128,0},{192,64},{1,129},{65,193},{129,1},{193,65... | collective-permute-start | bytes 196616 | tf_op jit(solution)/shard_map/ppermute | solution.py:156
  8.2 28.5 %all-to-all-start = ((bf16[32,64,128]{2,1,0:T(8,128)(2,1)}), bf16[32,64,128]{2,1,0:T(8,128)(2,1)S(1)}, u32[]{:S(2)}, u32[]{:S(2)}) async-start(bf16[32,64,128]{2,1,0:T(8,128)(2,1)} %bitcast.8), calls=%async_computation | async-start | bytes 1048576 | tf_op jit(solution)/shard_map/all_to_all | solution.py:151
  19.4 9.3 %collective-permute-start.5 = (bf16[4,2,128,128]{3,2,1,0:T(8,128)(2,1)S(1)}, bf16[4,2,128,128]{3,2,1,0:T(8,128)(2,1)S(1)}, u32[]{:S(2)}, u32[]{:S(2)}) collective-permute-start(bf16[4,2,128,128]{3,2,1,0:T(8,128)(2,1)S(1)} %pad_maximum_fusion.1.a0), channel_id=1, source_target_pairs={{48,0},{0,16},{16,32},{32,48},{49,1},{1,17},{17,33},{33,49},{50,2}... | collective-permute-start | bytes 786440 | tf_op jit(solution)/shard_map/ppermute | solution.py:158
  20.7 11.3 %collective-permute-start.4 = (bf16[4,2,128,128]{3,2,1,0:T(8,128)(2,1)S(1)}, bf16[4,2,128,128]{3,2,1,0:T(8,128)(2,1)S(1)}, u32[]{:S(2)}, u32[]{:S(2)}) collective-permute-start(bf16[4,2,128,128]{3,2,1,0:T(8,128)(2,1)S(1)} %pad_maximum_fusion.1.a0), channel_id=1, source_target_pairs={{32,0},{48,16},{0,32},{16,48},{33,1},{49,17},{1,33},{17,49},{34,2}... | collective-permute-start | bytes 786440 | tf_op jit(solution)/shard_map/ppermute | solution.py:158
  21.5 12.4 %collective-permute-start.3 = (bf16[4,2,128,128]{3,2,1,0:T(8,128)(2,1)S(1)}, bf16[4,2,128,128]{3,2,1,0:T(8,128)(2,1)S(1)}, u32[]{:S(2)}, u32[]{:S(2)}) collective-permute-start(bf16[4,2,128,128]{3,2,1,0:T(8,128)(2,1)S(1)} %pad_maximum_fusion.1.a0), channel_id=1, source_target_pairs={{16,0},{32,16},{48,32},{0,48},{17,1},{33,17},{49,33},{1,49},{18,2}... | collective-permute-start | bytes 786440 | tf_op jit(solution)/shard_map/ppermute | solution.py:158
  32.1 3.6 %collective-permute-start.7 = (bf16[8,2,128,128]{3,2,1,0:T(8,128)(2,1)S(1)}, bf16[8,2,128,128]{3,2,1,0:T(8,128)(2,1)S(1)}, u32[]{:S(2)}, u32[]{:S(2)}) collective-permute-start(bf16[8,2,128,128]{3,2,1,0:T(8,128)(2,1)S(1)} %pad_maximum_fusion), channel_id=1, source_target_pairs={{0,1},{1,0},{2,3},{3,2},{4,5},{5,4},{6,7},{7,6},{8,9},{9,8},{10,11... | collective-permute-start | bytes 1572872 | tf_op jit(solution)/shard_map/ppermute | solution.py:161
  34.6 0.7 copy-start.1
  34.6 2.1 %collective-permute-start.6 = (bf16[8,2,128,128]{3,2,1,0:T(8,128)(2,1)}, bf16[8,2,128,128]{3,2,1,0:T(8,128)(2,1)S(1)}, u32[]{:S(2)}, u32[]{:S(2)}) collective-permute-start(bf16[8,2,128,128]{3,2,1,0:T(8,128)(2,1)} %constant_dynamic-update-slice_fusion), channel_id=1, source_target_pairs={{0,1},{1,0},{2,3},{3,2},{4,5},{5,4},{6,7},{7,6},{8,9},{9,8},{10,11... | collective-permute-start | bytes 1572872 | tf_op jit(solution)/shard_map/ppermute | solution.py:160

commit v2 on v1

v2 whole, which is shorter than its diff:
```python
import math

import jax
import jax.numpy as jnp
from jax import lax
from jax.experimental import pallas as pl
from jax.experimental.pallas import tpu as pltpu
from jax.sharding import Mesh
from jax.sharding import PartitionSpec as P

HEADS = 64
GROUPS = 4
BLOCK = 128
HEADS_PER_GROUP = HEADS // GROUPS
SLOT_ROWS = 80
WIDTH=128
MASKED=-1e30
EXP_SCALE = math.log2(math.e) / math.sqrt(WIDTH)
VMEM = pl.BlockSpec(memory_space=pltpu.VMEM)
SMEM = pl.BlockSpec(memory_space=pltpu.SMEM)
def three_pieces(value):
    hi = value.astype(jnp.bfloat16).astype(jnp.float32)
    rest = value - hi
    mid = rest.astype(jnp.bfloat16).astype(jnp.float32)
    return hi, mid, rest - mid

def attend_half(scal, q_ref, kv, acc, m_scr, l_scr, steps, s_a, s_b, p_a, p_b, other):
    zl, x, core, x0 = scal[8], scal[9], scal[10], scal[11]
    c_at = core ^ 1 if other else core

    def fill(n, group, zl_at, lo, hi):
        steps[0, n] = group
        steps[1, n] = zl_at
        steps[2, n] = lo
        steps[3, n] = hi

    def scores(group, zl_at, s_ref):
        s = zl_at ^ zl
        keys = jnp.concatenate([kv(xr, s, 0) for xr in range(4)], axis=0)
        q = q_ref[pl.ds(pl.multiple_of(group * 512, 512), 512), :]
        s_ref[...] = lax.dot_general(keys, q, (((1,), (1,)), ((), ())), preferred_element_type=jnp.float32)

    def softmax(group, zl_at, lo, hi, s_ref, p_ref):
        base = c_at * 16 + zl_at * 4
        m_old = m_scr[group, 0:1, :]
        m_new = m_old
        bias = []
        for xr in range(4):
            at = base + ((x + xr) & 3)
            dead = (at < lo) | (at >= hi)
            bias.append(jnp.where(dead, jnp.float32(MASKED), jnp.float32(0.0)))
            top = jnp.max(s_ref[xr * 128 : (xr + 1) * 128, :], axis=0, keepdims=True)
            m_new = jnp.maximum(m_new, top + bias[xr])
        total = jnp.zeros((1, 512), jnp.float32)
        for xr in range(4):
            at = slice(xr * 128, (xr + 1) * 128)
            p = jnp.exp2((s_ref[at, :] - (m_new - bias[xr])) * EXP_SCALE)
            total = total + jnp.sum(p, axis=0, keepdims=True)
            p_ref[at, :] = p.astype(jnp.bfloat16)
        alpha = jnp.exp2((m_old - m_new) * EXP_SCALE)
        m_scr[group, 0:1, :] = m_new
        l_scr[group, 0:1, :] = l_scr[group, 0:1, :] * alpha + total
        s = zl_at ^ zl
        values = jnp.concatenate([kv(xr, s, 1) for xr in range(4)], axis=0)
        acc[group] = acc[group] * alpha + lax.dot_general(
            values, p_ref[...], (((0,), (0,)), ((), ())), preferred_element_type=jnp.float32)

    n = jnp.int32(0)
    for group in range(4):
        lo, hi, diagonal = scal[group], scal[4 + group], scal[12 + group]
        first = jnp.clip(lo - 16 * c_at, 0, 16)
        last = jnp.clip(hi - 16 * c_at, 0, 16)
        for zl_at in range(4):
            live = (first < zl_at * 4 + 4) & (last > zl_at * 4)
            at_diagonal = live & (diagonal >> 2 == c_at * 4 + zl_at)

            @pl.when(at_diagonal)
            def _():
                scores(group, zl_at, s_a)
                slot = pl.ds(pl.multiple_of(((diagonal - x) & 3) * 128, 128), 128)
                key = lax.broadcasted_iota(jnp.int32, (128, 512), 0)
                row = lax.broadcasted_iota(jnp.int32, (128, 512), 1)
                query = x0 * 64 + (row >> 6) * 8 + core * 4 + (row & 3)
                s_a[slot, :] = jnp.where(key <= query, s_a[slot, :], MASKED)
                softmax(group, zl_at, lo, hi, s_a, p_a)

            go = live & jnp.logical_not(at_diagonal)

            @pl.when(go)
            def _(n=n):
                fill(n, group, zl_at, lo, hi)

            n = n + go.astype(jnp.int32)

    @pl.when(n > 0)
    def _():
        for k in range(2):
            fill(n + k, steps[0, n - 1], steps[1, n - 1], 0, 0)

        def get(i):
            return steps[0, i], steps[1, i], steps[2, i], steps[3, i]

        g, z, _, _ = get(0)
        scores(g, z, s_a)

        def pair(i, carry):
            one, two, three = get(2 * i), get(2 * i + 1), get(2 * i + 2)
            scores(*two[:2], s_b)
            softmax(*one, s_a, p_a)
            scores(*three[:2], s_a)
            softmax(*two, s_b, p_b)
            return carry

        lax.fori_loop(0, (n + 1) // 2, pair, 0)

def attend_own(scal, q_ref, a0, a1, a2, a3, acc, m_scr, l_scr, steps, s_a, s_b, p_a, p_b):
    own = (a0, a1, a2, a3)
    m_scr[...] = jnp.full_like(m_scr, MASKED)
    l_scr[...] = jnp.zeros_like(l_scr)
    acc[...] = jnp.zeros_like(acc)
    attend_half(scal, q_ref, lambda xr, s, w: own[xr][s, w], acc, m_scr, l_scr, steps, s_a, s_b, p_a, p_b, False)

def attend_other(scal, q_ref, b0, b1, acc_in, m_in, l_in, out_ref, acc, m_scr, l_scr, steps, s_a, s_b, p_a, p_b):
    both = (b0, b1)
    m_scr[...] = m_in[...]
    l_scr[...] = l_in[...]
    acc[...] = acc_in[...]
    attend_half(scal, q_ref, lambda xr, s, w: both[xr // 2][(xr % 2) * 4 + s, w], acc, m_scr, l_scr, steps, s_a, s_b, p_a, p_b, True)
    for group in range(4):
        lo, hi = scal[group], scal[4 + group]

        @pl.when(lo < hi)
        def _():
            part = acc[group].T.astype(jnp.bfloat16)
            stats = (*three_pieces(m_scr[group, 0:1, :]), *three_pieces(l_scr[group, 0:1, :]))
            stats = jnp.concatenate([*stats, jnp.zeros((10, 512), jnp.float32)], axis=0)
            stats = stats.astype(jnp.bfloat16)
            for j in range(8):
                out_ref[group * 8 + j, 0:64, :] = part[j * 64 : (j + 1) * 64]
                out_ref[group * 8 + j, 64:80, :] = stats[:, (j // 2) * 128 : (j // 2 + 1) * 128]

        @pl.when(lo >= hi)
        def _():
            row = lax.broadcasted_iota(jnp.int32, (16, 128), 0)
            stats = jnp.where(row == 0, jnp.float32(MASKED), jnp.float32(0.0)).astype(jnp.bfloat16)
            for j in range(8):
                out_ref[group * 8 + j, 0:64, :] = jnp.zeros((64, 128), jnp.bfloat16)
                out_ref[group * 8 + j, 64:80, :] = stats
STATE=(jax.ShapeDtypeStruct((4,128,512),jnp.float32),jax.ShapeDtypeStruct((4,8,512),jnp.float32),jax.ShapeDtypeStruct((4,8,512),jnp.float32))
SCR=[pltpu.SMEM((4,32),jnp.int32),pltpu.VMEM((512,512),jnp.float32),pltpu.VMEM((512,512),jnp.float32),pltpu.VMEM((512,512),jnp.bfloat16),pltpu.VMEM((512,512),jnp.bfloat16)]
CP=pltpu.CompilerParams(vmem_limit_bytes=32*1024*1024)
COST=pl.CostEstimate(flops=2*2*1024*2048*128,bytes_accessed=4<<20,transcendentals=1024*2048)
def own_call(scal,q,a0,a1,a2,a3):
    return pl.pallas_call(attend_own,out_shape=STATE,in_specs=[SMEM]+[VMEM]*5,out_specs=(VMEM,)*3,scratch_shapes=SCR,compiler_params=CP,cost_estimate=COST,name="attend_own")(scal,q,a0,a1,a2,a3)
def other_call(scal,q,b0,b1,*state):
    return pl.pallas_call(attend_other,out_shape=jax.ShapeDtypeStruct((32,80,128),jnp.bfloat16),in_specs=[SMEM]+[VMEM]*6,out_specs=VMEM,
      scratch_shapes=[pltpu.VMEM(s.shape,s.dtype) for s in STATE]+SCR,compiler_params=CP,cost_estimate=COST,name="attend_other")(scal,q,b0,b1,*state)


def combine(scal, parts, out_ref):
    odd = scal[16] & 1
    for g in range(GROUPS):
        m, l = [], []
        for plane in range(8):
            st = parts[g * 8 + plane, 64:80, :].astype(jnp.float32)
            m.append(st[0:1] + st[1:2] + st[2:3])
            l.append(st[3:4] + st[4:5] + st[5:6])
        m, l = jnp.concatenate(m, axis=0), jnp.concatenate(l, axis=0)
        w = jnp.exp2((m - jnp.max(m, axis=0, keepdims=True)) * EXP_SCALE)
        w = w / jnp.sum(w * l, axis=0, keepdims=True)
        w = jnp.where(odd == 1, pltpu.roll(w, 64, 1), w)
        w = w.T
        total = jnp.zeros((64, 128), jnp.float32)
        for plane in range(8):
            part = parts[g * 8 + plane, 0:64, :].astype(jnp.float32)
            total = total + part * w[0:64, plane : plane + 1]
        for h in range(HEADS_PER_GROUP):
            at = (g * HEADS_PER_GROUP + h) * WIDTH
            out_ref[:, at : at + WIDTH] = total[h * 4 : (h + 1) * 4, :].astype(jnp.bfloat16)


def from_x(k):
    return [((i + k) % 4, i) for i in range(4)]


def per_device(queries, keys_values, doc_blocks):
    zl, x, zh, y, core = (lax.axis_index(a) for a in ("zl", "x", "zh", "y", "core"))
    planes = ("zl", "zh", "y")
    q = queries.reshape(4, GROUPS, HEADS_PER_GROUP, WIDTH).transpose(1, 2, 0, 3)
    q = q.reshape(GROUPS, 1, 64, WIDTH)
    q = jnp.broadcast_to(q, (GROUPS, 8, 64, WIDTH)).reshape(32, 64, WIDTH)
    q = lax.all_to_all(q, planes, 0, 0, tiled=True).reshape(2048, WIDTH)
    heads = keys_values.reshape(2, BLOCK, GROUPS, WIDTH).transpose(2, 0, 1, 3)
    pieces = [lax.dynamic_index_in_dim(heads, zl, 0, False)]
    for s in (1, 2, 3):
        piece = lax.dynamic_index_in_dim(heads, zl ^ s, 0, False)
        pieces.append(lax.ppermute(piece, "zl", [(i, i ^ s) for i in range(4)]))
    a0 = jnp.stack(pieces)
    a1, a2, a3 = (lax.ppermute(a0, "x", from_x(k)) for k in (1, 2, 3))
    swap = [(0, 1), (1, 0)]
    b0 = lax.ppermute(jnp.concatenate([a0, a1]), "core", swap)
    b1 = lax.ppermute(jnp.concatenate([a2, a3]), "core", swap)
    plane = zh * 4 + y
    query_block = 2 * jnp.arange(4, dtype=jnp.int32) + x // 2
    at = query_block * 32 + 31
    index = jnp.arange(256, dtype=jnp.int32)
    own_doc = jnp.sum(jnp.where(index[None] == at[:, None], doc_blocks[None], 0), axis=1)
    start = jnp.sum((doc_blocks[None] < own_doc[:, None]).astype(jnp.int32), axis=1)
    lo = jnp.clip(start - 32 * plane, 0, 32)
    hi = jnp.clip(at + 1 - 32 * plane, 0, 32)
    diagonal = at - 32 * plane
    mine = jnp.stack([zl, x, core, x % 2]).astype(jnp.int32)
    scal = jnp.concatenate([lo, hi, mine, diagonal, (zh * 4 + y)[None]]).astype(jnp.int32)

    state = own_call(scal, q, a0, a1, a2, a3)
    part = other_call(scal, q, b0, b1, *state)
    part = lax.all_to_all(part, planes, 0, 0, tiled=True)
    return pl.pallas_call(
        combine,
        out_shape=jax.ShapeDtypeStruct((4, HEADS * WIDTH), jnp.bfloat16),
        in_specs=[SMEM, VMEM],
        out_specs=VMEM,
        compiler_params=CP,
        name="combine",
    )(scal, part)


def solution(mesh):
    split = Mesh(mesh.devices.reshape(4, 4, 2, 4, 2), ("zl", "x", "zh", "y", "core"))
    in_specs = (
        P(("zl", "x", "zh", "y", "core"), None),
        P(None, ("zh", "y", "core", "zl", "x"), None),
        P(),
    )
    out_specs = P(("zl", "x", "zh", "y", "core"), None)
    return jax.shard_map(
        per_device, mesh=split, in_specs=in_specs, out_specs=out_specs, check_vma=False
    )
```

time: 80.1 us -> 78.5 us (0.980)
  the two profiles are of different devices: /device:TPU:4 before, /device:TPU:32 now
where the time goes in v2:
time: 78.5 us; the launch traced here: 78.7 us
  blocking collectives  33.8 us (43%)
  starting transfers between devices  20.9 us (27%)
  waiting for transfers between devices  10.4 us (13%)
  local copies, waits for them, and re-layouts  6.77 us (9%)
  Pallas kernels  6.26 us (8%)
    all_to_all x1, blocking collectives, per_device(): part = lax.all_to_all(part, planes, 0, 0, tiled=True)  33.8 us
    all_to_all x1, starting transfers between devices, per_device(): q = lax.all_to_all(q, planes, 0, 0, tiled=True).reshape(2048, WIDTH)  11.6 us
    ppermute x3, waiting for transfers between devices, per_device(): a1, a2, a3 = (lax.ppermute(a0, 'x', from_x(k)) for k in (1, 2, 3))  9.92 us
    ppermute x3, starting transfers between devices, per_device(): a1, a2, a3 = (lax.ppermute(a0, 'x', from_x(k)) for k in (1, 2, 3))  4.52 us
    ppermute x3, starting transfers between devices, per_device(): pieces.append(lax.ppermute(piece, 'zl', [(i, i ^ s) for i in range(4)]))  4.12 us
    unnamed x11, local copies, waits for them, and re-layouts  3.49 us
    pallas_call x1, Pallas kernels, other_call(): pl.pallas_call(attend_other, out_shape=jax.ShapeDtypeStruct((32, 80, 128)...  3.11 us
    pallas_call x1, Pallas kernels, per_device(): pl.pallas_call(combine, out_shape=jax.ShapeDtypeStruct((4, HEADS * WIDTH)...  2.15 us
  transfers between devices with their start and end apart: 9, of which 3 were waited for; matrix products, arithmetic and copies ran while one was open for 6% of the time, Pallas kernels for 1%

profile of v2, /device:TPU:32, one launch (start us, length us, event | category | flops | bytes accessed | tf_op | source)
XLA Modules:
  0.0 78.7 jit_solution(16770548310892782816)
XLA Ops:
  0.0 1.0 %reshape.33 = bf16[2,128,4,128]{3,2,1,0:T(4,128)(2,1)S(1)} reshape(bf16[2,128,512]{2,1,0:T(8,128)(2,1)} %param.4) | data formatting | bytes 524288 | tf_op jit(solution)/shard_map/reshape | solution.py:193
  1.0 0.5 constant_dynamic-slice_fusion.3
  1.6 1.9 %collective-permute-start = (bf16[2,128,128]{2,1,0:T(8,128)(2,1)S(1)}, bf16[2,128,128]{2,1,0:T(8,128)(2,1)S(1)}, u32[]{:S(2)}, u32[]{:S(2)}) collective-permute-start(bf16[2,128,128]{2,1,0:T(8,128)(2,1)S(1)} %bitcast.36), channel_id=1, source_target_pairs={{0,64},{64,0},{128,192},{192,128},{1,65},{65,1},{129,193},{193,129... | collective-permute-start | bytes 196616 | tf_op jit(solution)/shard_map/ppermute | solution.py:197
  3.6 1.6 %collective-permute-start.1 = (bf16[2,128,128]{2,1,0:T(8,128)(2,1)S(1)}, bf16[2,128,128]{2,1,0:T(8,128)(2,1)S(1)}, u32[]{:S(2)}, u32[]{:S(2)}) collective-permute-start(bf16[2,128,128]{2,1,0:T(8,128)(2,1)S(1)} %bitcast.37), channel_id=1, source_target_pairs={{0,128},{64,192},{128,0},{192,64},{1,129},{65,193},{129,1},{193,65... | collective-permute-start | bytes 196616 | tf_op jit(solution)/shard_map/ppermute | solution.py:197
  5.2 0.6 collective-permute-start.2
  5.8 0.3 copy-done
  6.0 0.9 %broadcast_in_dim.28 = bf16[4,8,64,128]{3,2,1,0:T(8,128)(2,1)} broadcast(bf16[4,64,128]{2,1,0:T(8,128)(2,1)S(1)} %bitcast.35), dimensions={0,2,3} | broadcast | bytes 589824 | tf_op jit(solution)/shard_map/broadcast_in_dim | solution.py:191
  6.9 11.6 %all-to-all-start = ((bf16[32,64,128]{2,1,0:T(8,128)(2,1)}), bf16[32,64,128]{2,1,0:T(8,128)(2,1)S(1)}, u32[]{:S(2)}, u32[]{:S(2)}) async-start(bf16[32,64,128]{2,1,0:T(8,128)(2,1)} %bitcast.8), calls=%async_computation | async-start | bytes 1048576 | tf_op jit(solution)/shard_map/all_to_all | solution.py:192
  18.6 0.6 constant_dynamic-update-slice_fusion.4
  19.2 0.7 copy-done.1
  19.9 0.2 select_reduce_fusion
  20.1 0.0 collective-permute-done
  20.1 0.0 collective-permute-done.1
  20.1 0.0 collective-permute-done.2
  20.2 2.8 %collective-permute-start.3 = (bf16[4,2,128,128]{3,2,1,0:T(8,128)(2,1)S(1)}, bf16[4,2,128,128]{3,2,1,0:T(8,128)(2,1)S(1)}, u32[]{:S(2)}, u32[]{:S(2)}) collective-permute-start(bf16[4,2,128,128]{3,2,1,0:T(8,128)(2,1)S(1)} %pad_maximum_fusion.1.a0), channel_id=1, source_target_pairs={{16,0},{32,16},{48,32},{0,48},{17,1},{33,17},{49,33},{1,49},{18,2}... | collective-permute-start | bytes 786440 | tf_op jit(solution)/shard_map/ppermute | solution.py:199
  23.0 0.8 %collective-permute-start.5 = (bf16[4,2,128,128]{3,2,1,0:T(8,128)(2,1)S(1)}, bf16[4,2,128,128]{3,2,1,0:T(8,128)(2,1)S(1)}, u32[]{:S(2)}, u32[]{:S(2)}) collective-permute-start(bf16[4,2,128,128]{3,2,1,0:T(8,128)(2,1)S(1)} %pad_maximum_fusion.1.a0), channel_id=1, source_target_pairs={{32,0},{48,16},{0,32},{16,48},{33,1},{49,17},{1,33},{17,49},{34,2}... | collective-permute-start | bytes 786440 | tf_op jit(solution)/shard_map/ppermute | solution.py:199
  23.8 0.9 %collective-permute-start.6 = (bf16[4,2,128,128]{3,2,1,0:T(8,128)(2,1)S(1)}, bf16[4,2,128,128]{3,2,1,0:T(8,128)(2,1)S(1)}, u32[]{:S(2)}, u32[]{:S(2)}) collective-permute-start(bf16[4,2,128,128]{3,2,1,0:T(8,128)(2,1)S(1)} %pad_maximum_fusion.1.a0), channel_id=1, source_target_pairs={{48,0},{0,16},{16,32},{32,48},{49,1},{1,17},{17,33},{33,49},{50,2}... | collective-permute-start | bytes 786440 | tf_op jit(solution)/shard_map/ppermute | solution.py:199
  24.7 0.6 constant_dynamic-update-slice_fusion.3
  25.3 0.6 constant_dynamic-update-slice_fusion.2
  25.9 0.6 constant_dynamic-update-slice_fusion.1
  26.6 7.2 %collective-permute-done.5.a2 = bf16[4,2,128,128]{3,2,1,0:T(8,128)(2,1)S(1)} collective-permute-done((bf16[4,2,128,128]{3,2,1,0:T(8,128)(2,1)S(1)}, bf16[4,2,128,128]{3,2,1,0:T(8,128)(2,1)S(1)}, u32[]{:S(2)}, u32[]{:S(2)}) %collective-permute-start.5) | collective-permute-done | bytes 262176 | tf_op jit(solution)/shard_map/ppermute | solution.py:199
  33.7 2.8 %collective-permute-done.6.a3 = bf16[4,2,128,128]{3,2,1,0:T(8,128)(2,1)S(1)} collective-permute-done((bf16[4,2,128,128]{3,2,1,0:T(8,128)(2,1)S(1)}, bf16[4,2,128,128]{3,2,1,0:T(8,128)(2,1)S(1)}, u32[]{:S(2)}, u32[]{:S(2)}) %collective-permute-start.6) | collective-permute-done | bytes 262176 | tf_op jit(solution)/shard_map/ppermute | solution.py:199
  36.5 0.1 collective-permute-start.7
  36.7 0.7 constant_dynamic-update-slice_fusion
  37.4 0.5 collective-permute-start.4
  37.9 0.2 convert_reduce_fusion
  38.1 0.1 concatenate.10.scal
  38.2 1.0 %attend_own.1 = (f32[4,128,512]{2,1,0:T(8,128)S(1)}, f32[4,8,512]{2,1,0:T(8,128)S(1)}, f32[4,8,512]{2,1,0:T(8,128)S(1)}) custom-call(s32[17]{0:T(128)S(1)} %concatenate.10.scal, bf16[2048,128]{1,0:T(8,128)(2,1)S(1)} %bitcast.30, bf16[4,2,128,128]{3,2,1,0:T(8,128)(2,1)S(1)} %pad_maximum_fusion.1.a0, bf16[4,2,128,128]{3,2,1,0:T(8,128)(2,1)S(1)} %collective-permute-done.3.a1, ...), custom_call_target="tpu_custom_call" | custom-call | flops 1073741824 | bytes 4194304 | tf_op jit(solution)/shard_map/attend_own/pallas_call | solution.py:154
  39.2 0.4 collective-permute-done.4.b0
  39.6 3.1 %attend_other.1 = bf16[32,80,128]{2,1,0:T(8,128)(2,1)S(1)} custom-call(s32[17]{0:T(128)S(1)} %concatenate.10.scal, bf16[2048,128]{1,0:T(8,128)(2,1)S(1)} %bitcast.31, bf16[8,2,128,128]{3,2,1,0:T(8,128)(2,1)S(1)} %collective-permute-done.4.b0, bf16[8,2,128,128]{3,2,1,0:T(8,128)(2,1)S(1)} %collective-permute-done.7.b1, ...), custom_call_target="tpu_custom_call" | custom-call | flops 1073741824 | bytes 4194304 | tf_op jit(solution)/shard_map/attend_other/pallas_call | solution.py:156
  42.7 33.8 %all_to_all.10.parts = bf16[32,80,128]{2,1,0:T(8,128)(2,1)S(1)} all-to-all(bf16[32,80,128]{2,1,0:T(8,128)(2,1)S(1)} %attend_other.1), channel_id=1, replica_groups=mesh['zl'=4,'x'=4,'zh'=2,'y'=4,'core'=2] {'zl','zh','y'}, dimensions={0} | all-to-all | bytes 1310720 | tf_op jit(solution)/shard_map/all_to_all | solution.py:217
  76.5 2.1 %combine.1 = bf16[4,8192]{1,0:T(4,128)(2,1)} custom-call(s32[17]{0:T(128)S(1)} %concatenate.10.scal, bf16[32,80,128]{2,1,0:T(8,128)(2,1)S(1)} %all_to_all.10.parts), custom_call_target="tpu_custom_call" | custom-call | tf_op jit(solution)/shard_map/combine/pallas_call | solution.py:218
  (13 shorter events, 0.2 us)
Async XLA Ops:
  1.6 18.5 %collective-permute-start = (bf16[2,128,128]{2,1,0:T(8,128)(2,1)S(1)}, bf16[2,128,128]{2,1,0:T(8,128)(2,1)S(1)}, u32[]{:S(2)}, u32[]{:S(2)}) collective-permute-start(bf16[2,128,128]{2,1,0:T(8,128)(2,1)S(1)} %bitcast.36), channel_id=1, source_target_pairs={{0,64},{64,0},{128,192},{192,128},{1,65},{65,1},{129,193},{193,129... | collective-permute-start | bytes 196616 | tf_op jit(solution)/shard_map/ppermute | solution.py:197
  3.6 16.5 %collective-permute-start.1 = (bf16[2,128,128]{2,1,0:T(8,128)(2,1)S(1)}, bf16[2,128,128]{2,1,0:T(8,128)(2,1)S(1)}, u32[]{:S(2)}, u32[]{:S(2)}) collective-permute-start(bf16[2,128,128]{2,1,0:T(8,128)(2,1)S(1)} %bitcast.37), channel_id=1, source_target_pairs={{0,128},{64,192},{128,0},{192,64},{1,129},{65,193},{129,1},{193,65... | collective-permute-start | bytes 196616 | tf_op jit(solution)/shard_map/ppermute | solution.py:197
  5.2 0.8 %copy-start = (bf16[4,8192]{1,0:T(4,128)(2,1)S(1)}, bf16[4,8192]{1,0:T(4,128)(2,1)}, u32[]{:S(2)}) copy-start(bf16[4,8192]{1,0:T(4,128)(2,1)} %param.3) | copy-start | bytes 196612
  5.2 14.9 %collective-permute-start.2 = (bf16[2,128,128]{2,1,0:T(8,128)(2,1)S(1)}, bf16[2,128,128]{2,1,0:T(8,128)(2,1)S(1)}, u32[]{:S(2)}, u32[]{:S(2)}) collective-permute-start(bf16[2,128,128]{2,1,0:T(8,128)(2,1)S(1)} %bitcast.38), channel_id=1, source_target_pairs={{0,192},{64,128},{128,64},{192,0},{1,193},{65,129},{129,65},{193,1... | collective-permute-start | bytes 196616 | tf_op jit(solution)/shard_map/ppermute | solution.py:197
  6.9 31.2 %all-to-all-start = ((bf16[32,64,128]{2,1,0:T(8,128)(2,1)}), bf16[32,64,128]{2,1,0:T(8,128)(2,1)S(1)}, u32[]{:S(2)}, u32[]{:S(2)}) async-start(bf16[32,64,128]{2,1,0:T(8,128)(2,1)} %bitcast.8), calls=%async_computation | async-start | bytes 1048576 | tf_op jit(solution)/shard_map/all_to_all | solution.py:192
  19.2 0.7 copy-start.1
  20.2 16.5 %collective-permute-start.3 = (bf16[4,2,128,128]{3,2,1,0:T(8,128)(2,1)S(1)}, bf16[4,2,128,128]{3,2,1,0:T(8,128)(2,1)S(1)}, u32[]{:S(2)}, u32[]{:S(2)}) collective-permute-start(bf16[4,2,128,128]{3,2,1,0:T(8,128)(2,1)S(1)} %pad_maximum_fusion.1.a0), channel_id=1, source_target_pairs={{16,0},{32,16},{48,32},{0,48},{17,1},{33,17},{49,33},{1,49},{18,2}... | collective-permute-start | bytes 786440 | tf_op jit(solution)/shard_map/ppermute | solution.py:199
  23.0 10.7 %collective-permute-start.5 = (bf16[4,2,128,128]{3,2,1,0:T(8,128)(2,1)S(1)}, bf16[4,2,128,128]{3,2,1,0:T(8,128)(2,1)S(1)}, u32[]{:S(2)}, u32[]{:S(2)}) collective-permute-start(bf16[4,2,128,128]{3,2,1,0:T(8,128)(2,1)S(1)} %pad_maximum_fusion.1.a0), channel_id=1, source_target_pairs={{32,0},{48,16},{0,32},{16,48},{33,1},{49,17},{1,33},{17,49},{34,2}... | collective-permute-start | bytes 786440 | tf_op jit(solution)/shard_map/ppermute | solution.py:199
  23.8 12.7 %collective-permute-start.6 = (bf16[4,2,128,128]{3,2,1,0:T(8,128)(2,1)S(1)}, bf16[4,2,128,128]{3,2,1,0:T(8,128)(2,1)S(1)}, u32[]{:S(2)}, u32[]{:S(2)}) collective-permute-start(bf16[4,2,128,128]{3,2,1,0:T(8,128)(2,1)S(1)} %pad_maximum_fusion.1.a0), channel_id=1, source_target_pairs={{48,0},{0,16},{16,32},{32,48},{49,1},{1,17},{17,33},{33,49},{50,2}... | collective-permute-start | bytes 786440 | tf_op jit(solution)/shard_map/ppermute | solution.py:199
  36.5 2.6 %collective-permute-start.7 = (bf16[8,2,128,128]{3,2,1,0:T(8,128)(2,1)S(1)}, bf16[8,2,128,128]{3,2,1,0:T(8,128)(2,1)S(1)}, u32[]{:S(2)}, u32[]{:S(2)}) collective-permute-start(bf16[8,2,128,128]{3,2,1,0:T(8,128)(2,1)S(1)} %pad_maximum_fusion), channel_id=1, source_target_pairs={{0,1},{1,0},{2,3},{3,2},{4,5},{5,4},{6,7},{7,6},{8,9},{9,8},{10,11... | collective-permute-start | bytes 1572872 | tf_op jit(solution)/shard_map/ppermute | solution.py:202
  37.4 2.2 %collective-permute-start.4 = (bf16[8,2,128,128]{3,2,1,0:T(8,128)(2,1)}, bf16[8,2,128,128]{3,2,1,0:T(8,128)(2,1)S(1)}, u32[]{:S(2)}, u32[]{:S(2)}) collective-permute-start(bf16[8,2,128,128]{3,2,1,0:T(8,128)(2,1)} %constant_dynamic-update-slice_fusion), channel_id=1, source_target_pairs={{0,1},{1,0},{2,3},{3,2},{4,5},{5,4},{6,7},{7,6},{8,9},{9,8},{10,11... | collective-permute-start | bytes 1572872 | tf_op jit(solution)/shard_map/ppermute | solution.py:201
